TPU v7x, 32 devices: a whole 2x2x4 slice. The times are simulated.
32 devices in a mesh: gx: 4 (over z), gy: 2 (over core), gz: 4 (over y, x).
Axes of the slice: x: 2, y: 2, z: 4, core: 2. Of those that a mesh axis runs over, the one named last changes fastest.
Arguments:
- right_side: float32 [32, 32, 512], P('gx', 'gy', 'gz'), may hold values from -8 to 8
- coefficient: float32 [32, 32, 512], P('gx', 'gy', 'gz'), may hold values from 0.05 to 2
Outputs:
- correction: float32 [32, 32, 512], P('gx', 'gy', 'gz')
All inputs are finite; a program needn't handle non-finite values.
Results may differ from a plain program's by a relative error of at most 0.00002.
Values sent between devices are 32-bit elements; how exact they have to be, the bound alone decides.
A program may use at most 64 MiB of HBM per device.

v0:
```python
import jax
import jax.numpy as jnp
from jax import lax
from jax.sharding import PartitionSpec as P

SWEEPS = 4


RELAX_WEIGHT = 0.8


def padded_2(shard, sides, width):
    for axis, dim in sides:
        peers, length = (lax.axis_size(axis), shard.shape[dim])
        up = [(i, (i + 1) % peers) for i in range(peers - 1)]
        down = [(j, i) for i, j in up]
        last = lax.slice_in_dim(shard, length - width, length, axis=dim)
        leading = lax.slice_in_dim(shard, 0, width, axis=dim)
        before = lax.ppermute(last, axis, up)
        after = lax.ppermute(leading, axis, down)
        shard = jnp.concatenate([before, shard, after], axis=dim)
    return shard


def restrict(values):
    return values.reshape(
        values.shape[0] // 2, 2, values.shape[1] // 2, 2, values.shape[2] // 2, 2
    ).mean(axis=(1, 3, 5))


def prolong(values):
    return jnp.repeat(jnp.repeat(jnp.repeat(values, 2, axis=0), 2, axis=1), 2, axis=2)


def neighbours(padded):
    beside_all = padded[2:, 1:-1, 1:-1] + padded[:-2, 1:-1, 1:-1]
    beside_all = beside_all + padded[1:-1, 2:, 1:-1] + padded[1:-1, :-2, 1:-1]
    return beside_all + padded[1:-1, 1:-1, 2:] + padded[1:-1, 1:-1, :-2]


def plane_term(residual, coefficient):
    return jnp.mean(residual, axis=(0, 1)) / jnp.mean(coefficient + 0.0625, axis=(0, 1))


def sweep_deep(extended, spacing_scale, inside_mask, depth_dims):
    residual = extended[0]
    diagonal = 6.0 * spacing_scale + extended[1]
    iterate = RELAX_WEIGHT * residual / diagonal * inside_mask
    for repeat in range(SWEEPS - 1):
        beside_all = neighbours(jnp.pad(iterate, 1))
        iterate = (
            iterate
            + RELAX_WEIGHT
            * (residual - (diagonal * iterate - spacing_scale * beside_all))
            / diagonal
        ) * inside_mask
    cropped = iterate
    for dimension in depth_dims:
        cropped = lax.slice_in_dim(
            cropped, SWEEPS - 1, cropped.shape[dimension] - (SWEEPS - 1), axis=dimension
        )
    return cropped


def inside_band(first_cell, local_length, whole_length):
    rim_depth = SWEEPS - 1
    position = first_cell + jnp.arange(-rim_depth, local_length + rim_depth, dtype=jnp.int32)
    return jnp.where((position >= 0) & (position < whole_length), 1.0, 0.0).astype(jnp.float32)


def per_device(right_side, coefficient):
    local_x, local_y, local_z = right_side.shape
    count_x = lax.axis_size("gx")
    count_y = lax.axis_size("gy")
    count_z = lax.axis_size("gz")
    spot_x = lax.axis_index("gx")
    spot_y = lax.axis_index("gy")
    spot_z = lax.axis_index("gz")
    residual_one = restrict(right_side)
    coeff_one = restrict(coefficient)
    residual_mid, coeff_mid = (
        lax.all_gather(residual_one, "gx", axis=0, tiled=True),
        lax.all_gather(coeff_one, "gx", axis=0, tiled=True),
    )
    residual_two, coeff_two = (
        lax.all_gather(restrict(residual_mid), "gy", axis=1, tiled=True),
        lax.all_gather(restrict(coeff_mid), "gy", axis=1, tiled=True),
    )
    rim_depth = SWEEPS - 1
    coarse_ext = padded_2(jnp.stack([residual_two, coeff_two]), (("gz", 3),), rim_depth)
    coarse_z = residual_two.shape[2]
    coarse_mask = inside_band(spot_z * coarse_z, coarse_z, coarse_z * count_z)[None, None, :]
    coarse_part = sweep_deep(coarse_ext, 0.0625, coarse_mask, (2,))
    middle_ext = padded_2(jnp.stack([residual_mid, coeff_mid]), (("gy", 2), ("gz", 3)), rim_depth)
    middle_y = residual_mid.shape[1]
    middle_z = residual_mid.shape[2]
    middle_mask = (
        inside_band(spot_y * middle_y, middle_y, middle_y * count_y)[None, :, None]
        * inside_band(spot_z * middle_z, middle_z, middle_z * count_z)[None, None, :]
    )
    middle_part = sweep_deep(middle_ext, 0.25, middle_mask, (1, 2))
    fine_ext = padded_2(
        jnp.stack([right_side, coefficient]), (("gx", 1), ("gy", 2), ("gz", 3)), rim_depth
    )
    fine_mask = (
        inside_band(spot_x * local_x, local_x, local_x * count_x)[:, None, None]
        * inside_band(spot_y * local_y, local_y, local_y * count_y)[None, :, None]
        * inside_band(spot_z * local_z, local_z, local_z * count_z)[None, None, :]
    )
    fine_part = sweep_deep(fine_ext, 1.0, fine_mask, (0, 1, 2))
    coarse_part = coarse_part + plane_term(residual_two, coeff_two)[None, None, :]
    coarse_own = lax.dynamic_slice_in_dim(
        coarse_part, spot_y * (local_y // 4), local_y // 4, axis=1
    )
    middle_total = middle_part + prolong(coarse_own)
    middle_own = lax.dynamic_slice_in_dim(
        middle_total, spot_x * (local_x // 2), local_x // 2, axis=0
    )
    return fine_part + prolong(middle_own)


def solution(mesh):
    in_specs = (P("gx", "gy", "gz"), P("gx", "gy", "gz"))
    out_specs = P("gx", "gy", "gz")
    return jax.shard_map(
        per_device, mesh=mesh, in_specs=in_specs, out_specs=out_specs, check_vma=False
    )
```

profile of v0, /device:TPU:0, one launch (start us, length us, event | category | flops | bytes accessed | tf_op | source)
XLA Modules:
  0.0 119.9 jit_solution(4451701442148706354)
XLA Ops:
  0.0 6.2 %reshape.161 = f32[4,2,8,2,64,2]{5,4,3,2,1,0:T(8,128)} reshape(f32[8,16,128]{2,1,0:T(8,128)} %param.2) | data formatting | bytes 131072 | tf_op jit(solution)/shard_map/reshape | solution.py:26
  6.3 2.6 %reduce_sum.54 = f32[4,8,64]{2,1,0:T(8,128)S(1)} reduce(f32[4,2,8,2,64,2]{5,4,3,2,1,0:T(8,128)} %reshape.161, f32[]{:T(128)} %constant.31.clone.1), dimensions={1,3,5}, to_apply=%region_0.0 | reduce | flops 14336 | bytes 73732 | tf_op jit(solution)/shard_map/reduce_sum | solution.py:28
  8.8 14.9 %all_gather.12 = f32[16,8,64]{2,1,0:T(8,128)S(1)} all-gather(f32[4,8,64]{2,1,0:T(8,128)S(1)} %broadcast_multiply_fusion.2), channel_id=1, replica_groups=mesh['gx'=4,'gy'=2,'gz'=4] {'gx'}, dimensions={0}, use_global_device_ids=true | all-gather | bytes 40960 | tf_op jit(solution)/shard_map/all_gather | solution.py:82
  23.7 5.5 %reshape.162 = f32[4,2,8,2,64,2]{5,4,3,2,1,0:T(8,128)} reshape(f32[8,16,128]{2,1,0:T(8,128)S(1)} %copy-done) | data formatting | bytes 131072 | tf_op jit(solution)/shard_map/reshape | solution.py:26
  29.2 2.5 %reduce_sum.55 = f32[4,8,64]{2,1,0:T(8,128)S(1)} reduce(f32[4,2,8,2,64,2]{5,4,3,2,1,0:T(8,128)} %reshape.162, f32[]{:T(128)} %constant.31.clone.1), dimensions={1,3,5}, to_apply=%region_1.0 | reduce | flops 14336 | bytes 73732 | tf_op jit(solution)/shard_map/reduce_sum | solution.py:28
  31.8 13.3 %all_gather.13 = f32[16,8,64]{2,1,0:T(8,128)S(1)} all-gather(f32[4,8,64]{2,1,0:T(8,128)S(1)} %broadcast_multiply_fusion.1), channel_id=1, replica_groups=mesh['gx'=4,'gy'=2,'gz'=4] {'gx'}, dimensions={0}, use_global_device_ids=true | all-gather | bytes 40960 | tf_op jit(solution)/shard_map/all_gather | solution.py:83
  45.2 1.3 %collective-permute-start.6 = (f32[2,16,3,64]{3,2,1,0:T(4,128)S(1)}, f32[2,16,3,64]{3,2,1,0:T(4,128)S(1)}, u32[]{:S(2)}, u32[]{:S(2)}) collective-permute-start(f32[2,16,3,64]{3,2,1,0:T(4,128)S(1)} %get-tuple-element.22), channel_id=1, source_target_pairs={{0,4},{1,5},{2,6},{3,7},{8,12},{9,13},{10,14},{11,15},{16,20},{17,... | collective-permute-start | bytes 73736 | tf_op jit(solution)/shard_map/ppermute | solution.py:19
  46.5 1.3 %collective-permute-start.7 = (f32[2,16,3,64]{3,2,1,0:T(4,128)S(1)}, f32[2,16,3,64]{3,2,1,0:T(4,128)S(1)}, u32[]{:S(2)}, u32[]{:S(2)}) collective-permute-start(f32[2,16,3,64]{3,2,1,0:T(4,128)S(1)} %get-tuple-element.21), channel_id=1, source_target_pairs={{4,0},{5,1},{6,2},{7,3},{12,8},{13,9},{14,10},{15,11},{20,16},{21,... | collective-permute-start | bytes 73736 | tf_op jit(solution)/shard_map/ppermute | solution.py:20
  47.8 3.5 %reshape.163 = f32[8,2,4,2,32,2]{5,4,3,2,1,0:T(8,128)} reshape(f32[16,8,64]{2,1,0:T(8,128)S(1)} %all_gather.12) | data formatting | bytes 65536 | tf_op jit(solution)/shard_map/reshape | solution.py:26
  51.3 2.1 %reshape.164 = f32[8,2,4,2,32,2]{5,4,3,2,1,0:T(8,128)S(1)} reshape(f32[16,8,64]{2,1,0:T(8,128)S(1)} %all_gather.13) | data formatting | bytes 65536 | tf_op jit(solution)/shard_map/reshape | solution.py:26
  53.4 1.8 %reduce_sum.56 = f32[8,4,32]{2,1,0:T(4,128)S(1)} reduce(f32[8,2,4,2,32,2]{5,4,3,2,1,0:T(8,128)} %reshape.163, f32[]{:T(128)} %constant.31.clone.1), dimensions={1,3,5}, to_apply=%region_2.0 | reduce | flops 7168 | bytes 36868 | tf_op jit(solution)/shard_map/reduce_sum | solution.py:28
  55.3 2.6 %all_gather.14 = f32[8,8,32]{2,0,1:T(8,128)S(1)} all-gather(f32[8,4,32]{2,0,1:T(8,128)S(1)} %copy_multiply_fusion.1), channel_id=1, replica_groups=mesh['gx'=4,'gy'=2,'gz'=4] {'gy'}, dimensions={1}, use_global_device_ids=true | all-gather | bytes 12288 | tf_op jit(solution)/shard_map/all_gather | solution.py:86
  58.1 1.8 %all_gather.15 = f32[8,8,32]{2,0,1:T(8,128)S(1)} all-gather(f32[8,4,32]{2,0,1:T(8,128)S(1)} %copy_multiply_fusion), channel_id=1, replica_groups=mesh['gx'=4,'gy'=2,'gz'=4] {'gy'}, dimensions={1}, use_global_device_ids=true | all-gather | bytes 12288 | tf_op jit(solution)/shard_map/all_gather | solution.py:87
  60.0 3.4 %collective-permute-start.10 = (f32[2,8,8,3]{3,1,2,0:T(8,128)S(1)}, f32[2,8,8,3]{3,1,2,0:T(8,128)S(1)}, u32[]{:S(2)}, u32[]{:S(2)}) collective-permute-start(f32[2,8,8,3]{3,1,2,0:T(8,128)S(1)} %get-tuple-element.27), channel_id=1, source_target_pairs={{0,1},{1,2},{2,3},{4,5},{5,6},{6,7},{8,9},{9,10},{10,11},{12,13},{... | collective-permute-start | bytes 4616 | tf_op jit(solution)/shard_map/ppermute | solution.py:19
  64.8 3.4 %collective-permute-start = (f32[2,3,16,128]{3,2,1,0:T(8,128)S(1)}, f32[2,3,16,128]{3,2,1,0:T(8,128)S(1)}, u32[]{:S(2)}, u32[]{:S(2)}) collective-permute-start(f32[2,3,16,128]{3,2,1,0:T(8,128)S(1)} %get-tuple-element.23), channel_id=1, source_target_pairs={{0,8},{8,16},{16,24},{1,9},{9,17},{17,25},{2,10},{10,18},{18,26},{... | collective-permute-start | bytes 147464 | tf_op jit(solution)/shard_map/ppermute | solution.py:19
  71.0 4.6 %collective-permute-start.8 = (f32[2,16,14,3]{3,1,2,0:T(8,128)S(1)}, f32[2,16,14,3]{3,1,2,0:T(8,128)S(1)}, u32[]{:S(2)}, u32[]{:S(2)}) collective-permute-start(f32[2,16,14,3]{3,1,2,0:T(8,128)S(1)} %get-tuple-element.17), channel_id=1, source_target_pairs={{0,1},{1,2},{2,3},{4,5},{5,6},{6,7},{8,9},{9,10},{10,11},{12,13},{... | collective-permute-start | bytes 16136 | tf_op jit(solution)/shard_map/ppermute | solution.py:19
  77.3 2.8 %collective-permute-done.8 = f32[2,16,14,3]{3,1,2,0:T(8,128)S(1)} collective-permute-done((f32[2,16,14,3]{3,1,2,0:T(8,128)S(1)}, f32[2,16,14,3]{3,1,2,0:T(8,128)S(1)}, u32[]{:S(2)}, u32[]{:S(2)}) %collective-permute-start.8) | collective-permute-done | bytes 5408 | tf_op jit(solution)/shard_map/ppermute | solution.py:19
  80.1 7.8 %collective-permute-done.9 = f32[2,16,14,3]{3,1,2,0:T(8,128)S(1)} collective-permute-done((f32[2,16,14,3]{3,1,2,0:T(8,128)S(1)}, f32[2,16,14,3]{3,1,2,0:T(8,128)S(1)}, u32[]{:S(2)}, u32[]{:S(2)}) %collective-permute-start.9) | collective-permute-done | bytes 5408 | tf_op jit(solution)/shard_map/ppermute | solution.py:20
  88.6 1.3 %collective-permute-start.2 = (f32[2,14,3,128]{3,0,2,1:T(2,128)S(1)}, f32[2,14,3,128]{3,0,2,1:T(2,128)S(1)}, u32[]{:S(2)}, u32[]{:S(2)}) collective-permute-start(f32[2,14,3,128]{3,0,2,1:T(2,128)S(1)} %copy.56), channel_id=1, source_target_pairs={{0,4},{1,5},{2,6},{3,7},{8,12},{9,13},{10,14},{11,15},{16,20},{17,... | collective-permute-start | bytes 129032 | tf_op jit(solution)/shard_map/ppermute | solution.py:19
  91.9 1.6 %collective-permute-done.3 = f32[2,14,3,128]{3,0,2,1:T(2,128)S(1)} collective-permute-done((f32[2,14,3,128]{3,0,2,1:T(2,128)S(1)}, f32[2,14,3,128]{3,0,2,1:T(2,128)S(1)}, u32[]{:S(2)}, u32[]{:S(2)}) %collective-permute-start.3) | collective-permute-done | bytes 43040 | tf_op jit(solution)/shard_map/ppermute | solution.py:20
  93.9 2.5 %collective-permute-start.4 = (f32[2,14,22,3]{3,0,2,1:T(2,128)S(1)}, f32[2,14,22,3]{3,0,2,1:T(2,128)S(1)}, u32[]{:S(2)}, u32[]{:S(2)}) collective-permute-start(f32[2,14,22,3]{3,0,2,1:T(2,128)S(1)} %get-tuple-element.13), channel_id=1, source_target_pairs={{0,1},{1,2},{2,3},{4,5},{5,6},{6,7},{8,9},{9,10},{10,11},{12,13},{... | collective-permute-start | bytes 22184 | tf_op jit(solution)/shard_map/ppermute | solution.py:19
  96.4 1.5 %collective-permute-start.5 = (f32[2,14,22,3]{3,0,2,1:T(2,128)S(1)}, f32[2,14,22,3]{3,0,2,1:T(2,128)S(1)}, u32[]{:S(2)}, u32[]{:S(2)}) collective-permute-start(f32[2,14,22,3]{3,0,2,1:T(2,128)S(1)} %get-tuple-element.14), channel_id=1, source_target_pairs={{1,0},{2,1},{3,2},{5,4},{6,5},{7,6},{9,8},{10,9},{11,10},{13,12},{... | collective-permute-start | bytes 22184 | tf_op jit(solution)/shard_map/ppermute | solution.py:20
  98.1 5.3 %collective-permute-done.4 = f32[2,14,22,3]{3,0,2,1:T(2,128)S(1)} collective-permute-done((f32[2,14,22,3]{3,0,2,1:T(2,128)S(1)}, f32[2,14,22,3]{3,0,2,1:T(2,128)S(1)}, u32[]{:S(2)}, u32[]{:S(2)}) %collective-permute-start.4) | collective-permute-done | bytes 7424 | tf_op jit(solution)/shard_map/ppermute | solution.py:19
  103.4 7.5 %collective-permute-done.5 = f32[2,14,22,3]{3,0,2,1:T(2,128)S(1)} collective-permute-done((f32[2,14,22,3]{3,0,2,1:T(2,128)S(1)}, f32[2,14,22,3]{3,0,2,1:T(2,128)S(1)}, u32[]{:S(2)}, u32[]{:S(2)}) %collective-permute-start.5) | collective-permute-done | bytes 7424 | tf_op jit(solution)/shard_map/ppermute | solution.py:20
  (91 shorter events, 18.1 us)
Async XLA Ops:
  6.3 17.5 %copy-start = (f32[8,16,128]{2,1,0:T(8,128)S(1)}, f32[8,16,128]{2,1,0:T(8,128)}, u32[]{:S(2)}) copy-start(f32[8,16,128]{2,1,0:T(8,128)} %param.3) | copy-start | bytes 196612
  45.2 25.7 %collective-permute-start.6 = (f32[2,16,3,64]{3,2,1,0:T(4,128)S(1)}, f32[2,16,3,64]{3,2,1,0:T(4,128)S(1)}, u32[]{:S(2)}, u32[]{:S(2)}) collective-permute-start(f32[2,16,3,64]{3,2,1,0:T(4,128)S(1)} %get-tuple-element.22), channel_id=1, source_target_pairs={{0,4},{1,5},{2,6},{3,7},{8,12},{9,13},{10,14},{11,15},{16,20},{17,... | collective-permute-start | bytes 73736 | tf_op jit(solution)/shard_map/ppermute | solution.py:19
  46.5 24.4 %collective-permute-start.7 = (f32[2,16,3,64]{3,2,1,0:T(4,128)S(1)}, f32[2,16,3,64]{3,2,1,0:T(4,128)S(1)}, u32[]{:S(2)}, u32[]{:S(2)}) collective-permute-start(f32[2,16,3,64]{3,2,1,0:T(4,128)S(1)} %get-tuple-element.21), channel_id=1, source_target_pairs={{4,0},{5,1},{6,2},{7,3},{12,8},{13,9},{14,10},{15,11},{20,16},{21,... | collective-permute-start | bytes 73736 | tf_op jit(solution)/shard_map/ppermute | solution.py:20
  57.9 6.9 %copy-start.1 = (f32[8,16,128]{2,1,0:T(8,128)S(1)}, f32[8,16,128]{2,1,0:T(8,128)}, u32[]{:S(2)}) copy-start(f32[8,16,128]{2,1,0:T(8,128)} %param.2) | copy-start | bytes 196612
  60.0 8.6 %collective-permute-start.10 = (f32[2,8,8,3]{3,1,2,0:T(8,128)S(1)}, f32[2,8,8,3]{3,1,2,0:T(8,128)S(1)}, u32[]{:S(2)}, u32[]{:S(2)}) collective-permute-start(f32[2,8,8,3]{3,1,2,0:T(8,128)S(1)} %get-tuple-element.27), channel_id=1, source_target_pairs={{0,1},{1,2},{2,3},{4,5},{5,6},{6,7},{8,9},{9,10},{10,11},{12,13},{... | collective-permute-start | bytes 4616 | tf_op jit(solution)/shard_map/ppermute | solution.py:19
  63.4 6.5 %collective-permute-start.11 = (f32[2,8,8,3]{3,1,2,0:T(8,128)S(1)}, f32[2,8,8,3]{3,1,2,0:T(8,128)S(1)}, u32[]{:S(2)}, u32[]{:S(2)}) collective-permute-start(f32[2,8,8,3]{3,1,2,0:T(8,128)S(1)} %get-tuple-element.28), channel_id=1, source_target_pairs={{1,0},{2,1},{3,2},{5,4},{6,5},{7,6},{9,8},{10,9},{11,10},{13,12},{... | collective-permute-start | bytes 4616 | tf_op jit(solution)/shard_map/ppermute | solution.py:20
  64.8 23.8 %collective-permute-start = (f32[2,3,16,128]{3,2,1,0:T(8,128)S(1)}, f32[2,3,16,128]{3,2,1,0:T(8,128)S(1)}, u32[]{:S(2)}, u32[]{:S(2)}) collective-permute-start(f32[2,3,16,128]{3,2,1,0:T(8,128)S(1)} %get-tuple-element.23), channel_id=1, source_target_pairs={{0,8},{8,16},{16,24},{1,9},{9,17},{17,25},{2,10},{10,18},{18,26},{... | collective-permute-start | bytes 147464 | tf_op jit(solution)/shard_map/ppermute | solution.py:19
  68.6 19.9 %collective-permute-start.1 = (f32[2,3,16,128]{3,2,1,0:T(8,128)S(1)}, f32[2,3,16,128]{3,2,1,0:T(8,128)S(1)}, u32[]{:S(2)}, u32[]{:S(2)}) collective-permute-start(f32[2,3,16,128]{3,2,1,0:T(8,128)S(1)} %get-tuple-element.24), channel_id=1, source_target_pairs={{8,0},{16,8},{24,16},{9,1},{17,9},{25,17},{10,2},{18,10},{26,18},{... | collective-permute-start | bytes 147464 | tf_op jit(solution)/shard_map/ppermute | solution.py:20
  71.0 9.1 %collective-permute-start.8 = (f32[2,16,14,3]{3,1,2,0:T(8,128)S(1)}, f32[2,16,14,3]{3,1,2,0:T(8,128)S(1)}, u32[]{:S(2)}, u32[]{:S(2)}) collective-permute-start(f32[2,16,14,3]{3,1,2,0:T(8,128)S(1)} %get-tuple-element.17), channel_id=1, source_target_pairs={{0,1},{1,2},{2,3},{4,5},{5,6},{6,7},{8,9},{9,10},{10,11},{12,13},{... | collective-permute-start | bytes 16136 | tf_op jit(solution)/shard_map/ppermute | solution.py:19
  75.6 12.3 %collective-permute-start.9 = (f32[2,16,14,3]{3,1,2,0:T(8,128)S(1)}, f32[2,16,14,3]{3,1,2,0:T(8,128)S(1)}, u32[]{:S(2)}, u32[]{:S(2)}) collective-permute-start(f32[2,16,14,3]{3,1,2,0:T(8,128)S(1)} %get-tuple-element.18), channel_id=1, source_target_pairs={{1,0},{2,1},{3,2},{5,4},{6,5},{7,6},{9,8},{10,9},{11,10},{13,12},{... | collective-permute-start | bytes 16136 | tf_op jit(solution)/shard_map/ppermute | solution.py:20
  88.6 3.0 %collective-permute-start.2 = (f32[2,14,3,128]{3,0,2,1:T(2,128)S(1)}, f32[2,14,3,128]{3,0,2,1:T(2,128)S(1)}, u32[]{:S(2)}, u32[]{:S(2)}) collective-permute-start(f32[2,14,3,128]{3,0,2,1:T(2,128)S(1)} %copy.56), channel_id=1, source_target_pairs={{0,4},{1,5},{2,6},{3,7},{8,12},{9,13},{10,14},{11,15},{16,20},{17,... | collective-permute-start | bytes 129032 | tf_op jit(solution)/shard_map/ppermute | solution.py:19
  90.3 3.1 %collective-permute-start.3 = (f32[2,14,3,128]{3,0,2,1:T(2,128)S(1)}, f32[2,14,3,128]{3,0,2,1:T(2,128)S(1)}, u32[]{:S(2)}, u32[]{:S(2)}) collective-permute-start(f32[2,14,3,128]{3,0,2,1:T(2,128)S(1)} %copy.57), channel_id=1, source_target_pairs={{4,0},{5,1},{6,2},{7,3},{12,8},{13,9},{14,10},{15,11},{20,16},{21,... | collective-permute-start | bytes 129032 | tf_op jit(solution)/shard_map/ppermute | solution.py:20
  93.9 9.5 %collective-permute-start.4 = (f32[2,14,22,3]{3,0,2,1:T(2,128)S(1)}, f32[2,14,22,3]{3,0,2,1:T(2,128)S(1)}, u32[]{:S(2)}, u32[]{:S(2)}) collective-permute-start(f32[2,14,22,3]{3,0,2,1:T(2,128)S(1)} %get-tuple-element.13), channel_id=1, source_target_pairs={{0,1},{1,2},{2,3},{4,5},{5,6},{6,7},{8,9},{9,10},{10,11},{12,13},{... | collective-permute-start | bytes 22184 | tf_op jit(solution)/shard_map/ppermute | solution.py:19
  96.4 14.5 %collective-permute-start.5 = (f32[2,14,22,3]{3,0,2,1:T(2,128)S(1)}, f32[2,14,22,3]{3,0,2,1:T(2,128)S(1)}, u32[]{:S(2)}, u32[]{:S(2)}) collective-permute-start(f32[2,14,22,3]{3,0,2,1:T(2,128)S(1)} %get-tuple-element.14), channel_id=1, source_target_pairs={{1,0},{2,1},{3,2},{5,4},{6,5},{7,6},{9,8},{10,9},{11,10},{13,12},{... | collective-permute-start | bytes 22184 | tf_op jit(solution)/shard_map/ppermute | solution.py:20
where the time goes:
time: 120 us
  blocking collectives  32.7 us (27%)
  waiting for transfers between devices  25 us (21%)
  starting transfers between devices  24.4 us (20%)
  local copies, waits for them, and re-layouts  23.3 us (19%)
  other arithmetic  14 us (12%)
    reshape x4, local copies, waits for them, and re-layouts, restrict(): values.reshape(values.shape[0] // 2, 2, values.shape[1] // 2, 2, values.s...  17.4 us
    ppermute x6, waiting for transfers between devices, padded_2(): after = lax.ppermute(leading, axis, down)  16.9 us
    ppermute x6, starting transfers between devices, padded_2(): before = lax.ppermute(last, axis, up)  16.4 us
    all_gather x1, blocking collectives, per_device(): lax.all_gather(residual_one, 'gx', axis=0, tiled=True)  14.9 us
    all_gather x1, blocking collectives, per_device(): lax.all_gather(coeff_one, 'gx', axis=0, tiled=True)  13.3 us
    ppermute x6, waiting for transfers between devices, padded_2(): before = lax.ppermute(last, axis, up)  8.11 us
    ppermute x6, starting transfers between devices, padded_2(): after = lax.ppermute(leading, axis, down)  7.93 us
    reduce_sum x4, other arithmetic, restrict(): return values.reshape(values.shape[0] // 2, 2, values.shape[1] // 2, 2, v...  7.16 us
  transfers between devices with their start and end apart: 12, of which 5 were waited for; matrix products, arithmetic and copies ran while one was open for 9% of the time, Pallas kernels for 0%

commit v1 on v0

v1 whole, which is shorter than its diff:
```python
import functools
import itertools

import jax
import jax.numpy as jnp
from jax import lax
from jax.experimental import pallas as pl
from jax.experimental.pallas import tpu as pltpu
from jax.sharding import PartitionSpec as P

SWEEPS = 4
RELAX_WEIGHT = 0.8
RIM = SWEEPS - 1

MESH = pl.DeviceIdType.MESH
LANES = 128
ROWS = 8
F32 = jnp.float32

MSG_TILES = 6
MSG_FINE = 2
MSG_TWO = 3
MSG_ONE = (0, 1, 4, 5)
MSG_SPAN = {-1: (0, 4), 0: (0, 6), 1: (2, 6)}


def dot(a, b):
    return jnp.dot(a, b, precision=lax.Precision.HIGHEST, preferred_element_type=F32)


def iota(shape, dim):
    return lax.broadcasted_iota(jnp.int32, shape, dim)


def lane_roll(values, shift):
    shift = shift % LANES
    return values if shift == 0 else pltpu.roll(values, shift, axis=values.ndim - 1)


def row_roll(values, shift):
    axis = values.ndim - 2
    return pltpu.roll(values, shift % values.shape[axis], axis=axis)


def terms(residual, coefficient, scale, mask):
    weight = RELAX_WEIGHT / (6.0 * scale + coefficient)
    return (
        jnp.where(mask, weight * residual, 0.0),
        jnp.where(mask, scale * weight, 0.0),
    )


def sweep_one_column(start, gain):
    value = start
    for _ in range(SWEEPS - 1):
        centre = value[1:-1]
        beside = value[2:] + value[:-2]
        beside = beside + (row_roll(centre, 1) + row_roll(centre, -1))
        beside = beside + (lane_roll(centre, 1) + lane_roll(centre, -1))
        start, gain = start[1:-1], gain[1:-1]
        value = (1.0 - RELAX_WEIGHT) * centre + start + gain * beside
    return value


def kernel(
    counts, extent, right_ref, coeff_ref, out_ref,
    fine, one, group, msg, zbox, pairs,
    load_sem, send_near, recv_near, send_one, recv_one, send_z, recv_z, send_two, recv_two,
):
    count_x, count_y, count_z = counts
    lx, ly, lz = extent
    x1 = lx // 2
    half = lz // 2
    quarter = lz // 4
    spot_x, spot_y, spot_z = (lax.axis_index(a) for a in ("gx", "gy", "gz"))

    def inside(dx, dy, dz):
        ok = None
        for spot, step, count in ((spot_x, dx, count_x), (spot_y, dy, count_y), (spot_z, dz, count_z)):
            if step == 0:
                continue
            here = (spot + step >= 0) & (spot + step < count)
            ok = here if ok is None else ok & here
        return ok

    near = [d for d in itertools.product((-1, 0, 1), repeat=2) if d != (0, 0)]
    along_z = [(dx, dy, dz) for dz in (-1, 1) for dx, dy in itertools.product((0, -1, 1), repeat=2)]
    peers = [p for p in itertools.product(range(count_x), range(count_y)) if p != (0, 0)]

    def target(dx, dy, dz):
        return (spot_x + dx, spot_y + dy, spot_z + dz)

    def peer_id(px, py):
        return (lax.rem(spot_x + px, count_x), lax.rem(spot_y + py, count_y), spot_z)

    barrier = pltpu.get_barrier_semaphore()
    for p in peers:
        pl.semaphore_signal(barrier, inc=1, device_id=peer_id(*p), device_id_type=MESH)
    expected = jnp.int32(len(peers))
    for d in along_z:
        ok = inside(*d)

        @pl.when(ok)
        def _(d=d):
            pl.semaphore_signal(barrier, inc=1, device_id=target(*d), device_id_type=MESH)

        expected = expected + ok.astype(jnp.int32)

    own = (slice(None), pl.ds(RIM, lx), pl.ds(ROWS, ly))
    loads = [
        pltpu.make_async_copy(ref, fine.at[i, pl.ds(RIM, lx), pl.ds(ROWS, ly)], load_sem.at[i])
        for i, ref in enumerate((right_ref, coeff_ref))
    ]
    for copy in loads:
        copy.start()
    for copy in loads:
        copy.wait()

    sums = []
    for i in range(2):
        planes = []
        for x in range(x1):
            total = None
            for a, b in itertools.product(range(2), range(2)):
                part = fine[i, RIM + 2 * x + a, pl.ds(ROWS + b, ly // 2, stride=2), :]
                total = part if total is None else total + part
            planes.append(total)
        for x in range(x1 // 2):
            pairs[i, pl.ds(x * ROWS, ROWS), :] = planes[2 * x] + planes[2 * x + 1]
        twos = pairs[i, pl.ds(0, ROWS, stride=2), :] + pairs[i, pl.ds(1, ROWS, stride=2), :]
        sums.append(jnp.concatenate(planes + [twos], axis=0))
    stacked = jnp.concatenate(sums, axis=1)
    shape = (2 * LANES, LANES)
    to_one = jnp.where(iota(shape, 1) == iota(shape, 0) // 2, 0.125, 0.0).astype(F32)
    to_two = jnp.where(iota(shape, 1) % (2 * quarter) == iota(shape, 0) // 4, 1.0 / 64, 0.0).astype(F32)
    coarse = dot(stacked, jnp.concatenate([to_one, to_two], axis=1))
    own_one = [coarse[x * ROWS:(x + 1) * ROWS, :LANES] for x in range(x1)]
    own_two = coarse[x1 * ROWS:, LANES:]
    my_slot = spot_x * count_y + spot_y
    group[my_slot] = own_two
    for x in range(x1):
        one[RIM + x, ROWS:2 * ROWS, :] = own_one[x]

    lane = iota((ROWS, LANES), 1)
    row = iota((ROWS, LANES), 0)
    place = lane % 8
    tiles_y = ly // ROWS
    pack_r = pack_c = None
    for k in range(lx * tiles_y):
        x, t = divmod(k, tiles_y)
        r = lane_roll(fine[0, RIM + x, pl.ds(ROWS * (1 + t), ROWS), :], 8 * k + 3)
        c = lane_roll(fine[1, RIM + x, pl.ds(ROWS * (1 + t), ROWS), :], 8 * k + 6)
        if pack_r is None:
            pack_r, pack_c = r, c
        else:
            pack_r = jnp.where(lane // 8 == k, r, pack_r)
            pack_c = jnp.where((lane + (LANES - 3)) % LANES // 8 == k, c, pack_c)
    high = jnp.where(place < 3, pack_r, pack_c)
    low = jnp.where((place >= 3) & (place < 6), pack_r, pack_c)
    for side, rim in enumerate((high, low)):
        msg[side, MSG_FINE] = rim
        msg[side, MSG_TWO] = own_two
        for x in range(x1):
            msg[side, MSG_ONE[x]] = own_one[x]

    pl.semaphore_wait(barrier, expected)

    flights = []

    def rim_range(step, size, rim, before):
        if step == 0:
            return pl.ds(before, size), pl.ds(before, size)
        if step < 0:
            return pl.ds(before, rim), pl.ds(before + size, rim)
        return pl.ds(before + size - rim, rim), pl.ds(before - rim, rim)

    for dx, dy in near:
        depth = RIM - abs(dy)
        i = (dx + 1) * 3 + dy + 1
        src_x, dst_x = rim_range(dx, lx, depth, RIM)
        src_y, dst_y = rim_range(dy, ly, ROWS, ROWS)
        flights.append((inside(dx, dy, 0), inside(-dx, -dy, 0), pltpu.make_async_remote_copy(
            src_ref=fine.at[:, src_x, src_y], dst_ref=fine.at[:, dst_x, dst_y],
            send_sem=send_near.at[i], recv_sem=recv_near.at[i],
            device_id=target(dx, dy, 0), device_id_type=MESH)))
        src_x, dst_x = rim_range(dx, x1, depth, RIM)
        src_y, dst_y = rim_range(dy, ROWS, ROWS, ROWS)
        flights.append((inside(dx, dy, 0), inside(-dx, -dy, 0), pltpu.make_async_remote_copy(
            src_ref=one.at[src_x, src_y], dst_ref=one.at[dst_x, dst_y],
            send_sem=send_one.at[i], recv_sem=recv_one.at[i],
            device_id=target(dx, dy, 0), device_id_type=MESH)))
    for dx, dy, dz in along_z:
        side = 0 if dz == 1 else 1
        i = (side * 3 + dx + 1) * 3 + dy + 1
        first, last = MSG_SPAN[dx]
        span = pl.ds(first, last - first)
        flights.append((inside(dx, dy, dz), inside(-dx, -dy, -dz), pltpu.make_async_remote_copy(
            src_ref=msg.at[side, span], dst_ref=zbox.at[side, 1 - dx, 1 - dy, span],
            send_sem=send_z.at[i], recv_sem=recv_z.at[i],
            device_id=target(dx, dy, dz), device_id_type=MESH)))
    for i, p in enumerate(peers):
        flights.append((None, None, pltpu.make_async_remote_copy(
            src_ref=group.at[my_slot], dst_ref=group.at[my_slot],
            send_sem=send_two.at[i], recv_sem=recv_two.at[i],
            device_id=peer_id(*p), device_id_type=MESH)))

    def guarded(condition, act):
        if condition is None:
            act()
        else:
            pl.when(condition)(act)

    for to, _, copy in flights:
        guarded(to, copy.start)
    for _, come, copy in flights:
        guarded(come, copy.wait_recv)
    for to, _, copy in flights:
        guarded(to, copy.wait_send)

    def open_side(spot, count, step):
        if step == 0:
            return jnp.bool_(True)
        return (spot + step >= 0) & (spot + step < count)

    def sides(position, low_end, high_start, spot, count):
        below = jnp.where(spot > 0, 0, low_end)
        above = jnp.where(spot < count - 1, 2 ** 20, high_start)
        return (position >= below) & (position < above)

    above_z = jnp.where(spot_z < count_z - 1, 1, 0)
    below_z = jnp.where(spot_z > 0, 1, 0)

    def lane_mask(shape, width, split):
        at = iota(shape, len(shape) - 1)
        allowed = jnp.where(at < width, 1, jnp.where(at < split, above_z, below_z))
        return allowed > 0

    def z_tile(side, dx, dy, tile):
        return zbox[side, dx + 1, dy + 1, tile]

    lower, upper = [], []
    for dx in range(-2, 3):
        tiles = []
        for dy in (-1, 0, 1):
            at = (jnp.clip(spot_x + dx, 0, count_x - 1) * count_y
                  + jnp.clip(spot_y + dy, 0, count_y - 1))
            tile = group[at]
            r, c = tile, lane_roll(tile, -quarter)
            if abs(dx) < 2:
                up, down = z_tile(1, dx, dy, MSG_TWO), z_tile(0, dx, dy, MSG_TWO)
                r = jnp.where(lane < quarter, r, lane_roll(jnp.where(lane >= 48, up, down), -quarter))
                c = jnp.where(lane < quarter, c, lane_roll(jnp.where(lane >= 80, up, down), -2 * quarter))
            ok = (spot_x + dx >= 0) & (spot_x + dx < count_x) & open_side(spot_y, count_y, dy)
            mask = lane_mask((ROWS, LANES), quarter, 80) & (jnp.where(ok, 1, 0) > 0)
            tiles.append(terms(r, c, 0.0625, mask))
        for x in range(2):
            lo, up_rows = [], []
            for j in range(2):
                before, mid, after = (t[j] for t in tiles)
                if x == 0:
                    lo.append(jnp.where(row < 4, before, row_roll(mid, 4)))
                    up_rows.append(after)
                else:
                    lo.append(jnp.where(row < 4, row_roll(before, 4), mid))
                    up_rows.append(row_roll(after, 4))
            lower.append(lo)
            upper.append(up_rows)
    start_two, gain_two = (
        jnp.stack([jnp.concatenate([lower[i][j], upper[i][j]], axis=0) for i in range(1, 9)])
        for j in range(2)
    )
    value_two = sweep_one_column(start_two, gain_two)[:, :ROWS]
    value_two = jnp.where(row < 4, row_roll(value_two[0], 4), value_two[1])
    total = group[0]
    for i in range(1, count_x * count_y):
        total = total + group[i]
    total = jnp.sum(total, axis=0, keepdims=True) * (1.0 / (count_x * count_y * ROWS))
    plane = total / (lane_roll(jnp.broadcast_to(total, (ROWS, LANES)), -quarter) + 0.0625)
    value_two = jnp.where(lane < quarter, value_two + plane, 0.0)

    empty = one[0, 0:ROWS, :]
    ups, downs = [], []
    for xe in range(x1 + 2 * RIM):
        x = xe - RIM
        up, down = [], []
        for dy in (-1, 0, 1):
            dx = -1 if x < 0 else (1 if x >= x1 else 0)
            if x < -2 or x >= x1 + 2:
                up.append(empty)
                down.append(empty)
                continue
            tile = MSG_ONE[x - dx * x1]
            up.append(z_tile(1, dx, dy, tile))
            down.append(z_tile(0, dx, dy, tile))
        ups.append(jnp.concatenate(up, axis=0))
        downs.append(jnp.concatenate(down, axis=0))
    up, down = jnp.stack(ups), jnp.stack(downs)
    block = one[...]
    shape = block.shape
    at = iota(shape, 2)
    r = jnp.where(at < half, block, lane_roll(jnp.where(at < 32, up, down), half))
    c = jnp.where(at < half, lane_roll(block, half), jnp.where(at < 96, up, down))
    mask = (
        lane_mask(shape, half, 96)
        & sides(iota(shape, 0), RIM, RIM + x1, spot_x, count_x)
        & sides(iota(shape, 1), ROWS, 2 * ROWS, spot_y, count_y)
    )
    value_one = sweep_one_column(*terms(r, c, 0.25, mask))[:, ROWS:2 * ROWS]
    value_one = jnp.where(iota(value_one.shape, 2) < half, value_one, 0.0)

    spread = jnp.concatenate(
        [value_one.reshape(x1 * ROWS, LANES), lane_roll(value_two, half)], axis=0)
    shape = (LANES, LANES)
    at, to = iota(shape, 0), iota(shape, 1)
    widen = jnp.where((at == to // 2) | (at - half == to // 4), 1.0, 0.0).astype(F32)
    spread = dot(spread, widen)
    shape = (lx * ly, (x1 + 1) * ROWS)
    at, to = iota(shape, 0), iota(shape, 1)
    x, y = at // ly, at % ly
    pick = (to == x // 2 * ROWS + y // 2) | (to - x1 * ROWS == x // 4 * 4 + y // 4)
    coarse_part = dot(jnp.where(pick, 1.0, 0.0).astype(F32), spread).reshape(lx, ly, LANES)

    rim_r, rim_c = [], []
    for xe in range(lx + 2 * RIM):
        x = xe - RIM
        if x < -2 or x >= lx + 2:
            pad = fine[0, xe]
            rim_r.append(pad)
            rim_c.append(pad)
            continue
        dx = -1 if x < 0 else (1 if x >= lx else 0)
        row_r, row_c = [], []
        for dy, t in [(-1, tiles_y - 1)] + [(0, t) for t in range(tiles_y)] + [(1, 0)]:
            k = (x - dx * lx) * tiles_y + t
            up, down = z_tile(1, dx, dy, MSG_FINE), z_tile(0, dx, dy, MSG_FINE)
            row_r.append(lane_roll(jnp.where(place < 3, down, up), -8 * k - 3))
            row_c.append(lane_roll(jnp.where((place >= 3) & (place < 6), down, up), -8 * k - 6))
        rim_r.append(jnp.concatenate(row_r, axis=0))
        rim_c.append(jnp.concatenate(row_c, axis=0))
    shape = (lx + 2 * RIM, ly + 2 * ROWS, LANES)
    mask = (
        sides(iota(shape, 0), RIM, RIM + lx, spot_x, count_x)
        & sides(iota(shape, 1), ROWS, ROWS + ly, spot_y, count_y)
    )
    start, gain = terms(fine[0], fine[1], 1.0, mask)
    start_rim, gain_rim = terms(
        jnp.stack(rim_r), jnp.stack(rim_c), 1.0, mask & lane_mask(shape, 0, 64))
    value, value_rim = start, start_rim
    for step in range(SWEEPS - 1):
        def beside(v):
            centre = v[1:-1]
            return v[2:] + v[:-2] + (row_roll(centre, 1) + row_roll(centre, -1))

        near_main, near_rim = beside(value), beside(value_rim)
        start, gain, value = start[1:-1], gain[1:-1], value[1:-1]
        start_rim, gain_rim, value_rim = start_rim[1:-1], gain_rim[1:-1], value_rim[1:-1]
        at = iota(value.shape, 2)
        right, right_rim = lane_roll(value, -1), lane_roll(value_rim, -1)
        left, left_rim = lane_roll(value, 1), lane_roll(value_rim, 1)
        is_last, is_first = at == LANES - 1, at == 0
        near_main = near_main + jnp.where(is_last, right_rim, right) + jnp.where(is_first, left_rim, left)
        near_rim = near_rim + jnp.where(is_last, right, right_rim) + jnp.where(is_first, left, left_rim)
        value = (1.0 - RELAX_WEIGHT) * value + start + gain * near_main
        value_rim = (1.0 - RELAX_WEIGHT) * value_rim + start_rim + gain_rim * near_rim
    out_ref[...] = value[:, ROWS:ROWS + ly] + coarse_part


def per_device(counts, right_side, coefficient):
    lx, ly, lz = right_side.shape
    assert lx // 4 == 2 and ly == 2 * ROWS and lz == LANES
    slots = counts[0] * counts[1]
    dma = pltpu.SemaphoreType.DMA
    return pl.pallas_call(
        functools.partial(kernel, counts, (lx, ly, lz)),
        out_shape=jax.ShapeDtypeStruct(right_side.shape, F32),
        in_specs=[pl.BlockSpec(memory_space=pl.ANY)] * 2,
        out_specs=pl.BlockSpec(memory_space=pltpu.VMEM),
        scratch_shapes=[
            pltpu.VMEM((2, lx + 2 * RIM, ly + 2 * ROWS, LANES), F32),
            pltpu.VMEM((lx // 2 + 2 * RIM, 3 * ROWS, LANES), F32),
            pltpu.VMEM((slots, ROWS, LANES), F32),
            pltpu.VMEM((2, MSG_TILES, ROWS, LANES), F32),
            pltpu.VMEM((2, 3, 3, MSG_TILES, ROWS, LANES), F32),
            pltpu.VMEM((2, 2 * ROWS, LANES), F32),
            dma((2,)),
            dma((9,)), dma((9,)), dma((9,)), dma((9,)),
            dma((18,)), dma((18,)),
            dma((max(slots - 1, 1),)), dma((max(slots - 1, 1),)),
        ],
        compiler_params=pltpu.CompilerParams(
            collective_id=0, has_side_effects=True, vmem_limit_bytes=32 * 1024 * 1024
        ),
    )(right_side, coefficient)


def solution(mesh):
    spec = P("gx", "gy", "gz")
    counts = tuple(mesh.shape[a] for a in ("gx", "gy", "gz"))
    return jax.shard_map(
        functools.partial(per_device, counts), mesh=mesh, in_specs=(spec, spec), out_specs=spec,
        check_vma=False,
    )
```

time: 120 us -> 15.2 us (0.13)
  blocking collectives: 32.7 us -> 0 us
  waiting for transfers between devices: 25 us -> 0 us
  starting transfers between devices: 24.4 us -> 0 us
  local copies, waits for them, and re-layouts: 23.3 us -> 2.31 us
  other arithmetic: 14 us -> 0 us
  Pallas kernels: 0 us -> 12.6 us
    all_gather x4 -> x0, blocking collectives: 32.7 us -> none  [the longest x1 14.9 us: per_device(): lax.all_gather(residual_one, 'gx', axis=0, tiled=True)]
    ppermute x12 -> x0, waiting for transfers between devices: 25 us -> none  [the longest x6 16.9 us: padded_2(): after = lax.ppermute(leading, axis, down)]
    ppermute x12 -> x0, starting transfers between devices: 24.4 us -> none  [the longest x6 16.4 us: padded_2(): before = lax.ppermute(last, axis, up)]
    reshape x6 -> x0, local copies, waits for them, and re-layouts: 17.6 us -> none  [the longest x4 17.4 us: restrict(): values.reshape(values.shape[0] // 2, 2, values.shape[1] // 2, 2, values.s...]
    pallas_call x0 -> x1, Pallas kernels: none -> 12.6 us  [per_device(): pl.pallas_call(functools.partial(kernel, counts, (lx, ly, lz)), out_shape...]
    reduce_sum x6 -> x0, other arithmetic: 7.22 us -> none  [the longest x4 7.16 us: restrict(): return values.reshape(values.shape[0] // 2, 2, values.shape[1] // 2, 2, v...]
    mul x13 -> x0, other arithmetic: 3.32 us -> none  [the longest x3 1.42 us: sweep_deep(): diagonal * iterate - spacing_scale * beside_all]
    add x5 -> x0, other arithmetic: 1.7 us -> none  [the longest x1 0.91 us: per_device(): return fine_part + prolong(middle_own)]
  transfers between devices with their start and end apart: 12 -> 0, of which waited for: 5 -> 0; matrix products, arithmetic and copies ran while one was open for 9% -> 0% of each run, Pallas kernels for 0% -> 0%
where the time goes in v1:
time: 15.2 us; the launch traced here: 15 us
  Pallas kernels  12.6 us (83%)
  local copies, waits for them, and re-layouts  2.31 us (15%)
    pallas_call x1, Pallas kernels, per_device(): pl.pallas_call(functools.partial(kernel, counts, (lx, ly, lz)), out_shape...  12.6 us
    unnamed x5, local copies, waits for them, and re-layouts  2.31 us

profile of v1, /device:TPU:0, one launch (start us, length us, event | category | flops | bytes accessed | tf_op | source)
XLA Modules:
  0.0 15.0 jit_solution(18243277033429206449)
XLA Ops:
  0.0 0.0 copy-start
  0.0 0.8 %copy-done = f32[8,16,128]{2,1,0:T(8,128)S(1)} copy-done((f32[8,16,128]{2,1,0:T(8,128)S(1)}, f32[8,16,128]{2,1,0:T(8,128)}, u32[]{:S(2)}) %copy-start) | copy-done | bytes 65560
  0.8 0.0 copy-start.1
  0.8 0.8 %copy-done.1 = f32[8,16,128]{2,1,0:T(8,128)S(1)} copy-done((f32[8,16,128]{2,1,0:T(8,128)S(1)}, f32[8,16,128]{2,1,0:T(8,128)}, u32[]{:S(2)}) %copy-start.1) | copy-done | bytes 65560
  1.7 12.6 %shard_map.28 = f32[8,16,128]{2,1,0:T(8,128)S(1)} custom-call(f32[8,16,128]{2,1,0:T(8,128)S(1)} %copy-done, f32[8,16,128]{2,1,0:T(8,128)S(1)} %copy-done.1), custom_call_target="tpu_custom_call" | custom-call | tf_op jit(solution)/shard_map/pallas_call | solution.py:373
  14.3 0.6 %copy.4 = f32[8,16,128]{2,1,0:T(8,128)} copy(f32[8,16,128]{2,1,0:T(8,128)S(1)} %shard_map.28) | data formatting | bytes 131072
Async XLA Ops:
  0.0 0.8 %copy-start = (f32[8,16,128]{2,1,0:T(8,128)S(1)}, f32[8,16,128]{2,1,0:T(8,128)}, u32[]{:S(2)}) copy-start(f32[8,16,128]{2,1,0:T(8,128)} %right_ref.1) | copy-start | bytes 196612
  0.8 0.8 %copy-start.1 = (f32[8,16,128]{2,1,0:T(8,128)S(1)}, f32[8,16,128]{2,1,0:T(8,128)}, u32[]{:S(2)}) copy-start(f32[8,16,128]{2,1,0:T(8,128)} %coeff_ref.1) | copy-start | bytes 196612

commit v2 on v1

--- a/solution.py
+++ b/solution.py
@@ -17,11 +17,9 @@
 ROWS = 8
 F32 = jnp.float32
 
-MSG_TILES = 6
-MSG_FINE = 2
-MSG_TWO = 3
-MSG_ONE = (0, 1, 4, 5)
-MSG_SPAN = {-1: (0, 4), 0: (0, 6), 1: (2, 6)}
+MSG_TILES = 2
+MSG_FINE = 0
+MSG_COARSE = 1
 
 
 def dot(a, b):
@@ -157,15 +155,18 @@
             pack_c = jnp.where((lane + (LANES - 3)) % LANES // 8 == k, c, pack_c)
     high = jnp.where(place < 3, pack_r, pack_c)
     low = jnp.where((place >= 3) & (place < 6), pack_r, pack_c)
+    rims = own_one[0]
+    for x in range(1, x1):
+        rims = jnp.where((lane + 3) % half // 8 == x, lane_roll(own_one[x], 8 * x), rims)
+    rims = jnp.where((lane >= 27) & (lane < 61), own_two, rims)
+    rims = jnp.where((lane >= 91) & (lane < 125), lane_roll(own_two, quarter), rims)
     for side, rim in enumerate((high, low)):
         msg[side, MSG_FINE] = rim
-        msg[side, MSG_TWO] = own_two
-        for x in range(x1):
-            msg[side, MSG_ONE[x]] = own_one[x]
+        msg[side, MSG_COARSE] = rims
 
     pl.semaphore_wait(barrier, expected)
 
-    flights = []
+    flights_fine, flights_one, flights_z, flights_two = [], [], [], []
 
     def rim_range(step, size, rim, before):
         if step == 0:
@@ -179,27 +180,25 @@
         i = (dx + 1) * 3 + dy + 1
         src_x, dst_x = rim_range(dx, lx, depth, RIM)
         src_y, dst_y = rim_range(dy, ly, ROWS, ROWS)
-        flights.append((inside(dx, dy, 0), inside(-dx, -dy, 0), pltpu.make_async_remote_copy(
+        flights_fine.append((inside(dx, dy, 0), inside(-dx, -dy, 0), pltpu.make_async_remote_copy(
             src_ref=fine.at[:, src_x, src_y], dst_ref=fine.at[:, dst_x, dst_y],
             send_sem=send_near.at[i], recv_sem=recv_near.at[i],
             device_id=target(dx, dy, 0), device_id_type=MESH)))
         src_x, dst_x = rim_range(dx, x1, depth, RIM)
         src_y, dst_y = rim_range(dy, ROWS, ROWS, ROWS)
-        flights.append((inside(dx, dy, 0), inside(-dx, -dy, 0), pltpu.make_async_remote_copy(
+        flights_one.append((inside(dx, dy, 0), inside(-dx, -dy, 0), pltpu.make_async_remote_copy(
             src_ref=one.at[src_x, src_y], dst_ref=one.at[dst_x, dst_y],
             send_sem=send_one.at[i], recv_sem=recv_one.at[i],
             device_id=target(dx, dy, 0), device_id_type=MESH)))
     for dx, dy, dz in along_z:
         side = 0 if dz == 1 else 1
         i = (side * 3 + dx + 1) * 3 + dy + 1
-        first, last = MSG_SPAN[dx]
-        span = pl.ds(first, last - first)
-        flights.append((inside(dx, dy, dz), inside(-dx, -dy, -dz), pltpu.make_async_remote_copy(
-            src_ref=msg.at[side, span], dst_ref=zbox.at[side, 1 - dx, 1 - dy, span],
+        flights_z.append((inside(dx, dy, dz), inside(-dx, -dy, -dz), pltpu.make_async_remote_copy(
+            src_ref=msg.at[side], dst_ref=zbox.at[side, 1 - dx, 1 - dy],
             send_sem=send_z.at[i], recv_sem=recv_z.at[i],
             device_id=target(dx, dy, dz), device_id_type=MESH)))
     for i, p in enumerate(peers):
-        flights.append((None, None, pltpu.make_async_remote_copy(
+        flights_two.append((None, None, pltpu.make_async_remote_copy(
             src_ref=group.at[my_slot], dst_ref=group.at[my_slot],
             send_sem=send_two.at[i], recv_sem=recv_two.at[i],
             device_id=peer_id(*p), device_id_type=MESH)))
@@ -210,12 +209,14 @@
         else:
             pl.when(condition)(act)
 
+    def arrive(flights):
+        for _, come, copy in flights:
+            guarded(come, copy.wait_recv)
+
+    flights_two.reverse()
+    flights = flights_two + flights_z + flights_one + flights_fine
     for to, _, copy in flights:
         guarded(to, copy.start)
-    for _, come, copy in flights:
-        guarded(come, copy.wait_recv)
-    for to, _, copy in flights:
-        guarded(to, copy.wait_send)
 
     def open_side(spot, count, step):
         if step == 0:
@@ -237,6 +238,9 @@
 
     def z_tile(side, dx, dy, tile):
         return zbox[side, dx + 1, dy + 1, tile]
+
+    arrive(flights_two)
+    arrive(flights_z)
 
     lower, upper = [], []
     for dx in range(-2, 3):
@@ -247,9 +251,11 @@
             tile = group[at]
             r, c = tile, lane_roll(tile, -quarter)
             if abs(dx) < 2:
-                up, down = z_tile(1, dx, dy, MSG_TWO), z_tile(0, dx, dy, MSG_TWO)
-                r = jnp.where(lane < quarter, r, lane_roll(jnp.where(lane >= 48, up, down), -quarter))
-                c = jnp.where(lane < quarter, c, lane_roll(jnp.where(lane >= 80, up, down), -2 * quarter))
+                up, down = z_tile(1, dx, dy, MSG_COARSE), z_tile(0, dx, dy, MSG_COARSE)
+                r_rim = jnp.where(lane < half, lane_roll(up, half), lane_roll(down, -quarter))
+                c_rim = jnp.where(lane < half, up, lane_roll(down, quarter))
+                r = jnp.where(lane < quarter, r, r_rim)
+                c = jnp.where(lane < quarter, c, c_rim)
             ok = (spot_x + dx >= 0) & (spot_x + dx < count_x) & open_side(spot_y, count_y, dy)
             mask = lane_mask((ROWS, LANES), quarter, 80) & (jnp.where(ok, 1, 0) > 0)
             tiles.append(terms(r, c, 0.0625, mask))
@@ -278,28 +284,27 @@
     plane = total / (lane_roll(jnp.broadcast_to(total, (ROWS, LANES)), -quarter) + 0.0625)
     value_two = jnp.where(lane < quarter, value_two + plane, 0.0)
 
-    empty = one[0, 0:ROWS, :]
-    ups, downs = [], []
+    arrive(flights_one)
+    both = {
+        (dx, dy): jnp.where(place < 4, z_tile(1, dx, dy, MSG_COARSE), z_tile(0, dx, dy, MSG_COARSE))
+        for dx, dy in itertools.product((-1, 0, 1), repeat=2)
+    }
+    rim_r, rim_c = [], []
     for xe in range(x1 + 2 * RIM):
         x = xe - RIM
-        up, down = [], []
-        for dy in (-1, 0, 1):
-            dx = -1 if x < 0 else (1 if x >= x1 else 0)
-            if x < -2 or x >= x1 + 2:
-                up.append(empty)
-                down.append(empty)
-                continue
-            tile = MSG_ONE[x - dx * x1]
-            up.append(z_tile(1, dx, dy, tile))
-            down.append(z_tile(0, dx, dy, tile))
-        ups.append(jnp.concatenate(up, axis=0))
-        downs.append(jnp.concatenate(down, axis=0))
-    up, down = jnp.stack(ups), jnp.stack(downs)
+        dx = -1 if x < 0 else (1 if x >= x1 else 0)
+        at = 8 * (x - dx * x1)
+        if x < -2 or x >= x1 + 2:
+            rim_r.append(one[xe])
+            rim_c.append(one[xe])
+            continue
+        rim_r.append(jnp.concatenate([lane_roll(both[dx, dy], half - at) for dy in (-1, 0, 1)], axis=0))
+        rim_c.append(jnp.concatenate([lane_roll(both[dx, dy], -at) for dy in (-1, 0, 1)], axis=0))
     block = one[...]
     shape = block.shape
     at = iota(shape, 2)
-    r = jnp.where(at < half, block, lane_roll(jnp.where(at < 32, up, down), half))
-    c = jnp.where(at < half, lane_roll(block, half), jnp.where(at < 96, up, down))
+    r = jnp.where(at < half, block, jnp.stack(rim_r))
+    c = jnp.where(at < half, lane_roll(block, half), jnp.stack(rim_c))
     mask = (
         lane_mask(shape, half, 96)
         & sides(iota(shape, 0), RIM, RIM + x1, spot_x, count_x)
@@ -319,6 +324,8 @@
     x, y = at // ly, at % ly
     pick = (to == x // 2 * ROWS + y // 2) | (to - x1 * ROWS == x // 4 * 4 + y // 4)
     coarse_part = dot(jnp.where(pick, 1.0, 0.0).astype(F32), spread).reshape(lx, ly, LANES)
+
+    arrive(flights_fine)
 
     rim_r, rim_c = [], []
     for xe in range(lx + 2 * RIM):
@@ -363,6 +370,8 @@
         value = (1.0 - RELAX_WEIGHT) * value + start + gain * near_main
         value_rim = (1.0 - RELAX_WEIGHT) * value_rim + start_rim + gain_rim * near_rim
     out_ref[...] = value[:, ROWS:ROWS + ly] + coarse_part
+    for to, _, copy in flights:
+        guarded(to, copy.wait_send)
 
 
 def per_device(counts, right_side, coefficient):
@@ -373,7 +382,7 @@
     return pl.pallas_call(
         functools.partial(kernel, counts, (lx, ly, lz)),
         out_shape=jax.ShapeDtypeStruct(right_side.shape, F32),
-        in_specs=[pl.BlockSpec(memory_space=pl.ANY)] * 2,
+        in_specs=[pl.BlockSpec(memory_space=pltpu.HBM)] * 2,
         out_specs=pl.BlockSpec(memory_space=pltpu.VMEM),
         scratch_shapes=[
             pltpu.VMEM((2, lx + 2 * RIM, ly + 2 * ROWS, LANES), F32),

time: 15.2 us -> 13.7 us (0.901)
  Pallas kernels: 12.6 us -> 11.2 us
    pallas_call x1, Pallas kernels: 12.6 us -> 11.2 us  [per_device(): pl.pallas_call(functools.partial(kernel, counts, (lx, ly, lz)), out_shape...]
where the time goes in v2:
time: 13.7 us; the launch traced here: 13.5 us
  Pallas kernels  11.2 us (82%)
  local copies, waits for them, and re-layouts  2.31 us (17%)
    pallas_call x1, Pallas kernels, per_device(): pl.pallas_call(functools.partial(kernel, counts, (lx, ly, lz)), out_shape...  11.2 us
    unnamed x5, local copies, waits for them, and re-layouts  2.31 us

profile of v2, /device:TPU:0, one launch (start us, length us, event | category | flops | bytes accessed | tf_op | source)
XLA Modules:
  0.0 13.5 jit_solution(112122049724605233)
XLA Ops:
  0.0 0.0 copy-start
  0.0 0.8 %copy-done = f32[8,16,128]{2,1,0:T(8,128)S(1)} copy-done((f32[8,16,128]{2,1,0:T(8,128)S(1)}, f32[8,16,128]{2,1,0:T(8,128)}, u32[]{:S(2)}) %copy-start) | copy-done | bytes 65560
  0.8 0.0 copy-start.1
  0.8 0.8 %copy-done.1 = f32[8,16,128]{2,1,0:T(8,128)S(1)} copy-done((f32[8,16,128]{2,1,0:T(8,128)S(1)}, f32[8,16,128]{2,1,0:T(8,128)}, u32[]{:S(2)}) %copy-start.1) | copy-done | bytes 65560
  1.7 11.2 %shard_map.28 = f32[8,16,128]{2,1,0:T(8,128)S(1)} custom-call(f32[8,16,128]{2,1,0:T(8,128)S(1)} %copy-done, f32[8,16,128]{2,1,0:T(8,128)S(1)} %copy-done.1), custom_call_target="tpu_custom_call" | custom-call | tf_op jit(solution)/shard_map/pallas_call | solution.py:382
  12.9 0.6 %copy.4 = f32[8,16,128]{2,1,0:T(8,128)} copy(f32[8,16,128]{2,1,0:T(8,128)S(1)} %shard_map.28) | data formatting | bytes 131072
Async XLA Ops:
  0.0 0.8 %copy-start = (f32[8,16,128]{2,1,0:T(8,128)S(1)}, f32[8,16,128]{2,1,0:T(8,128)}, u32[]{:S(2)}) copy-start(f32[8,16,128]{2,1,0:T(8,128)} %right_ref.1) | copy-start | bytes 196612
  0.8 0.8 %copy-start.1 = (f32[8,16,128]{2,1,0:T(8,128)S(1)}, f32[8,16,128]{2,1,0:T(8,128)}, u32[]{:S(2)}) copy-start(f32[8,16,128]{2,1,0:T(8,128)} %coeff_ref.1) | copy-start | bytes 196612

commit v3 on v2

--- a/solution.py
+++ b/solution.py
@@ -11,6 +11,7 @@
 SWEEPS = 4
 RELAX_WEIGHT = 0.8
 RIM = SWEEPS - 1
+REACH = 2
 
 MESH = pl.DeviceIdType.MESH
 LANES = 128
@@ -62,8 +63,8 @@
 
 def kernel(
     counts, extent, right_ref, coeff_ref, out_ref,
-    fine, one, group, msg, zbox, pairs,
-    load_sem, send_near, recv_near, send_one, recv_one, send_z, recv_z, send_two, recv_two,
+    fine, one, group, msg, zbox, pairs, far,
+    load_sem, send_near, recv_near, send_one, recv_one, send_z, recv_z, send_two, recv_two, far_sem,
 ):
     count_x, count_y, count_z = counts
     lx, ly, lz = extent
@@ -83,19 +84,23 @@
 
     near = [d for d in itertools.product((-1, 0, 1), repeat=2) if d != (0, 0)]
     along_z = [(dx, dy, dz) for dz in (-1, 1) for dx, dy in itertools.product((0, -1, 1), repeat=2)]
-    peers = [p for p in itertools.product(range(count_x), range(count_y)) if p != (0, 0)]
+    reach = REACH if count_x <= 2 * REACH else count_x - 1
+    relayed = count_x > reach + 1
+    peers = [
+        (dx, dy)
+        for dx, dy in itertools.product(range(-reach, reach + 1), range(1 - count_y, count_y))
+        if (dx, dy) != (0, 0) and abs(dx) < count_x
+    ]
 
     def target(dx, dy, dz):
         return (spot_x + dx, spot_y + dy, spot_z + dz)
 
-    def peer_id(px, py):
-        return (lax.rem(spot_x + px, count_x), lax.rem(spot_y + py, count_y), spot_z)
-
     barrier = pltpu.get_barrier_semaphore()
-    for p in peers:
-        pl.semaphore_signal(barrier, inc=1, device_id=peer_id(*p), device_id_type=MESH)
-    expected = jnp.int32(len(peers))
-    for d in along_z:
+    greet = {(dx, dy, 0) for dx, dy in near + peers} | set(along_z)
+    expected = jnp.int32(0)
+    for d in sorted(greet, key=lambda d: (-abs(d[0]) - abs(d[2]), d)):
+        if abs(d[1]) >= count_y or abs(d[0]) >= count_x:
+            continue
         ok = inside(*d)
 
         @pl.when(ok)
@@ -103,8 +108,6 @@
             pl.semaphore_signal(barrier, inc=1, device_id=target(*d), device_id_type=MESH)
 
         expected = expected + ok.astype(jnp.int32)
-
-    own = (slice(None), pl.ds(RIM, lx), pl.ds(ROWS, ly))
     loads = [
         pltpu.make_async_copy(ref, fine.at[i, pl.ds(RIM, lx), pl.ds(ROWS, ly)], load_sem.at[i])
         for i, ref in enumerate((right_ref, coeff_ref))
@@ -166,7 +169,7 @@
 
     pl.semaphore_wait(barrier, expected)
 
-    flights_fine, flights_one, flights_z, flights_two = [], [], [], []
+    flights_fine, flights_one, flights_z, flights_two = [], [], [], {True: [], False: []}
 
     def rim_range(step, size, rim, before):
         if step == 0:
@@ -197,11 +200,16 @@
             src_ref=msg.at[side], dst_ref=zbox.at[side, 1 - dx, 1 - dy],
             send_sem=send_z.at[i], recv_sem=recv_z.at[i],
             device_id=target(dx, dy, dz), device_id_type=MESH)))
-    for i, p in enumerate(peers):
-        flights_two.append((None, None, pltpu.make_async_remote_copy(
+    for i, (dx, dy) in enumerate(peers):
+        flights_two[abs(dx) == 1].append((inside(dx, dy, 0), inside(-dx, -dy, 0), pltpu.make_async_remote_copy(
             src_ref=group.at[my_slot], dst_ref=group.at[my_slot],
             send_sem=send_two.at[i], recv_sem=recv_two.at[i],
-            device_id=peer_id(*p), device_id_type=MESH)))
+            device_id=target(dx, dy, 0), device_id_type=MESH)))
+    is_relay = (spot_x == reach) | (spot_x == count_x - 1 - reach)
+    is_end = (spot_x == 0) | (spot_x == count_x - 1)
+    relay = pltpu.make_async_remote_copy(
+        src_ref=far.at[0], dst_ref=far.at[1], send_sem=far_sem.at[0], recv_sem=far_sem.at[1],
+        device_id=(jnp.where(spot_x == reach, 0, count_x - 1), spot_y, spot_z), device_id_type=MESH)
 
     def guarded(condition, act):
         if condition is None:
@@ -213,8 +221,7 @@
         for _, come, copy in flights:
             guarded(come, copy.wait_recv)
 
-    flights_two.reverse()
-    flights = flights_two + flights_z + flights_one + flights_fine
+    flights = flights_two[True] + flights_two[False] + flights_z + flights_one + flights_fine
     for to, _, copy in flights:
         guarded(to, copy.start)
 
@@ -239,7 +246,18 @@
     def z_tile(side, dx, dy, tile):
         return zbox[side, dx + 1, dy + 1, tile]
 
-    arrive(flights_two)
+    arrive(flights_two[True])
+    if relayed:
+        @pl.when(is_relay)
+        def _():
+            end = jnp.where(spot_x == reach, count_x - 1, 0) * count_y
+            sums = group[end]
+            for i in range(1, count_y):
+                sums = sums + group[end + i]
+            far[0] = sums
+            relay.start()
+
+    arrive(flights_two[False])
     arrive(flights_z)
 
     lower, upper = [], []
@@ -277,12 +295,7 @@
     )
     value_two = sweep_one_column(start_two, gain_two)[:, :ROWS]
     value_two = jnp.where(row < 4, row_roll(value_two[0], 4), value_two[1])
-    total = group[0]
-    for i in range(1, count_x * count_y):
-        total = total + group[i]
-    total = jnp.sum(total, axis=0, keepdims=True) * (1.0 / (count_x * count_y * ROWS))
-    plane = total / (lane_roll(jnp.broadcast_to(total, (ROWS, LANES)), -quarter) + 0.0625)
-    value_two = jnp.where(lane < quarter, value_two + plane, 0.0)
+    value_two = jnp.where(lane < quarter, value_two, 0.0)
 
     arrive(flights_one)
     both = {
@@ -369,7 +382,26 @@
         near_rim = near_rim + jnp.where(is_last, right, right_rim) + jnp.where(is_first, left, left_rim)
         value = (1.0 - RELAX_WEIGHT) * value + start + gain * near_main
         value_rim = (1.0 - RELAX_WEIGHT) * value_rim + start_rim + gain_rim * near_rim
-    out_ref[...] = value[:, ROWS:ROWS + ly] + coarse_part
+    fine_part = value[:, ROWS:ROWS + ly] + coarse_part
+
+    total = None
+    for x in range(count_x):
+        part = group[x * count_y]
+        for i in range(1, count_y):
+            part = part + group[x * count_y + i]
+        if relayed:
+            part = jnp.where(jnp.abs(spot_x - x) <= reach, part, 0.0)
+        total = part if total is None else total + part
+    if relayed:
+        pl.when(is_end)(relay.wait_recv)
+        total = total + jnp.where(is_end, far[1], 0.0)
+    total = jnp.sum(total, axis=0, keepdims=True) * (1.0 / (count_x * count_y * ROWS))
+    total = jnp.broadcast_to(total, (ROWS, LANES))
+    plane = jnp.where(lane < quarter, total / (lane_roll(total, -quarter) + 0.0625), 0.0)
+    plane = dot(plane, jnp.where(iota((LANES, LANES), 0) == iota((LANES, LANES), 1) // 4, 1.0, 0.0).astype(F32))
+    out_ref[...] = fine_part + plane[0:1][None]
+    if relayed:
+        pl.when(is_relay)(relay.wait_send)
     for to, _, copy in flights:
         guarded(to, copy.wait_send)
 
@@ -391,10 +423,11 @@
             pltpu.VMEM((2, MSG_TILES, ROWS, LANES), F32),
             pltpu.VMEM((2, 3, 3, MSG_TILES, ROWS, LANES), F32),
             pltpu.VMEM((2, 2 * ROWS, LANES), F32),
+            pltpu.VMEM((2, ROWS, LANES), F32),
             dma((2,)),
             dma((9,)), dma((9,)), dma((9,)), dma((9,)),
             dma((18,)), dma((18,)),
-            dma((max(slots - 1, 1),)), dma((max(slots - 1, 1),)),
+            dma((4 * slots,)), dma((4 * slots,)), dma((2,)),
         ],
         compiler_params=pltpu.CompilerParams(
             collective_id=0, has_side_effects=True, vmem_limit_bytes=32 * 1024 * 1024

time: 13.7 us -> 14.5 us (1.058)
  Pallas kernels: 11.2 us -> 12 us
    pallas_call x1, Pallas kernels: 11.2 us -> 12 us  [per_device(): pl.pallas_call(functools.partial(kernel, counts, (lx, ly, lz)), out_shape...]
where the time goes in v3:
time: 14.5 us; the launch traced here: 14.3 us
  Pallas kernels  12 us (83%)
  local copies, waits for them, and re-layouts  2.31 us (16%)
    pallas_call x1, Pallas kernels, per_device(): pl.pallas_call(functools.partial(kernel, counts, (lx, ly, lz)), out_shape...  12 us
    unnamed x5, local copies, waits for them, and re-layouts  2.31 us

profile of v3, /device:TPU:0, one launch (start us, length us, event | category | flops | bytes accessed | tf_op | source)
XLA Modules:
  0.0 14.3 jit_solution(7928494335385313875)
XLA Ops:
  0.0 0.0 copy-start
  0.0 0.8 %copy-done = f32[8,16,128]{2,1,0:T(8,128)S(1)} copy-done((f32[8,16,128]{2,1,0:T(8,128)S(1)}, f32[8,16,128]{2,1,0:T(8,128)}, u32[]{:S(2)}) %copy-start) | copy-done | bytes 65560
  0.8 0.0 copy-start.1
  0.8 0.8 %copy-done.1 = f32[8,16,128]{2,1,0:T(8,128)S(1)} copy-done((f32[8,16,128]{2,1,0:T(8,128)S(1)}, f32[8,16,128]{2,1,0:T(8,128)}, u32[]{:S(2)}) %copy-start.1) | copy-done | bytes 65560
  1.7 12.0 %shard_map.28 = f32[8,16,128]{2,1,0:T(8,128)S(1)} custom-call(f32[8,16,128]{2,1,0:T(8,128)S(1)} %copy-done, f32[8,16,128]{2,1,0:T(8,128)S(1)} %copy-done.1), custom_call_target="tpu_custom_call" | custom-call | tf_op jit(solution)/shard_map/pallas_call | solution.py:414
  13.7 0.6 %copy.4 = f32[8,16,128]{2,1,0:T(8,128)} copy(f32[8,16,128]{2,1,0:T(8,128)S(1)} %shard_map.28) | data formatting | bytes 131072
Async XLA Ops:
  0.0 0.8 %copy-start = (f32[8,16,128]{2,1,0:T(8,128)S(1)}, f32[8,16,128]{2,1,0:T(8,128)}, u32[]{:S(2)}) copy-start(f32[8,16,128]{2,1,0:T(8,128)} %right_ref.1) | copy-start | bytes 196612
  0.8 0.8 %copy-start.1 = (f32[8,16,128]{2,1,0:T(8,128)S(1)}, f32[8,16,128]{2,1,0:T(8,128)}, u32[]{:S(2)}) copy-start(f32[8,16,128]{2,1,0:T(8,128)} %coeff_ref.1) | copy-start | bytes 196612

commit v4 on v2

--- a/solution.py
+++ b/solution.py
@@ -92,7 +92,7 @@
         return (lax.rem(spot_x + px, count_x), lax.rem(spot_y + py, count_y), spot_z)
 
     barrier = pltpu.get_barrier_semaphore()
-    for p in peers:
+    for p in sorted(peers, key=lambda p: -min(p[0], count_x - p[0])):
         pl.semaphore_signal(barrier, inc=1, device_id=peer_id(*p), device_id_type=MESH)
     expected = jnp.int32(len(peers))
     for d in along_z:
@@ -325,13 +325,11 @@
     pick = (to == x // 2 * ROWS + y // 2) | (to - x1 * ROWS == x // 4 * 4 + y // 4)
     coarse_part = dot(jnp.where(pick, 1.0, 0.0).astype(F32), spread).reshape(lx, ly, LANES)
 
-    arrive(flights_fine)
-
     rim_r, rim_c = [], []
     for xe in range(lx + 2 * RIM):
         x = xe - RIM
         if x < -2 or x >= lx + 2:
-            pad = fine[0, xe]
+            pad = jnp.zeros((ly + 2 * ROWS, LANES), F32)
             rim_r.append(pad)
             rim_c.append(pad)
             continue
@@ -349,9 +347,10 @@
         sides(iota(shape, 0), RIM, RIM + lx, spot_x, count_x)
         & sides(iota(shape, 1), ROWS, ROWS + ly, spot_y, count_y)
     )
-    start, gain = terms(fine[0], fine[1], 1.0, mask)
     start_rim, gain_rim = terms(
         jnp.stack(rim_r), jnp.stack(rim_c), 1.0, mask & lane_mask(shape, 0, 64))
+    arrive(flights_fine)
+    start, gain = terms(fine[0], fine[1], 1.0, mask)
     value, value_rim = start, start_rim
     for step in range(SWEEPS - 1):
         def beside(v):

time: 13.7 us -> 13.6 us (level)
  no operation moved by 1% of the time
where the time goes in v4:
time: 13.6 us; the launch traced here: 13.4 us
  Pallas kernels  11.1 us (82%)
  local copies, waits for them, and re-layouts  2.31 us (17%)
    pallas_call x1, Pallas kernels, per_device(): pl.pallas_call(functools.partial(kernel, counts, (lx, ly, lz)), out_shape...  11.1 us
    unnamed x5, local copies, waits for them, and re-layouts  2.31 us

profile of v4, /device:TPU:0, one launch (start us, length us, event | category | flops | bytes accessed | tf_op | source)
XLA Modules:
  0.0 13.4 jit_solution(682690253231445819)
XLA Ops:
  0.0 0.0 copy-start
  0.0 0.8 %copy-done = f32[8,16,128]{2,1,0:T(8,128)S(1)} copy-done((f32[8,16,128]{2,1,0:T(8,128)S(1)}, f32[8,16,128]{2,1,0:T(8,128)}, u32[]{:S(2)}) %copy-start) | copy-done | bytes 65560
  0.8 0.0 copy-start.1
  0.8 0.8 %copy-done.1 = f32[8,16,128]{2,1,0:T(8,128)S(1)} copy-done((f32[8,16,128]{2,1,0:T(8,128)S(1)}, f32[8,16,128]{2,1,0:T(8,128)}, u32[]{:S(2)}) %copy-start.1) | copy-done | bytes 65560
  1.7 11.1 %shard_map.28 = f32[8,16,128]{2,1,0:T(8,128)S(1)} custom-call(f32[8,16,128]{2,1,0:T(8,128)S(1)} %copy-done, f32[8,16,128]{2,1,0:T(8,128)S(1)} %copy-done.1), custom_call_target="tpu_custom_call" | custom-call | tf_op jit(solution)/shard_map/pallas_call | solution.py:381
  12.8 0.6 %copy.4 = f32[8,16,128]{2,1,0:T(8,128)} copy(f32[8,16,128]{2,1,0:T(8,128)S(1)} %shard_map.28) | data formatting | bytes 131072
Async XLA Ops:
  0.0 0.8 %copy-start = (f32[8,16,128]{2,1,0:T(8,128)S(1)}, f32[8,16,128]{2,1,0:T(8,128)}, u32[]{:S(2)}) copy-start(f32[8,16,128]{2,1,0:T(8,128)} %right_ref.1) | copy-start | bytes 196612
  0.8 0.8 %copy-start.1 = (f32[8,16,128]{2,1,0:T(8,128)S(1)}, f32[8,16,128]{2,1,0:T(8,128)}, u32[]{:S(2)}) copy-start(f32[8,16,128]{2,1,0:T(8,128)} %coeff_ref.1) | copy-start | bytes 196612
